TPU v7x, 512 devices: a whole 4x8x8 slice. The times are simulated.
512 devices in a mesh: ctx: 128 (over z, y, core), tp: 4 (over x).
Axes of the slice: x: 4, y: 8, z: 8, core: 2. Of those that a mesh axis runs over, the one named last changes fastest.
Arguments:
- queries: bfloat16 [65536, 4096], P('ctx', 'tp'), may hold values from -9 to 9
- keys: bfloat16 [65536, 512], P('ctx', 'tp'), may hold values from -9 to 9
- values: bfloat16 [65536, 512], P('ctx', 'tp'), may hold values from -6 to 6
- output_gradient: bfloat16 [65536, 4096], P('ctx', 'tp'), may hold values from -6 to 6
- doc_start: int32 [65536], P('ctx'), may hold values from 0 to 65535, as said below
Outputs:
- attended: bfloat16 [65536, 4096], P(('ctx', 'tp'))
- query_gradient: bfloat16 [65536, 4096], P('ctx', 'tp')
- key_gradient: bfloat16 [65536, 512], P('ctx', 'tp')
- value_gradient: bfloat16 [65536, 512], P('ctx', 'tp')
Inputs may be any that keep to these rules, and one draw needn't show every extreme that they name: doc_start[i] is the first position of the document holding position i; it never falls along the sequence, and no document crosses a multiple of 512. The shards of 512 positions are matched in pairs, shard s with shard s plus half the number of shards: documents in one of a pair are cut at a rate complementary to the other's, so a shard of long documents is matched with a shard of short ones.
All inputs are finite; a program needn't handle non-finite values.
Results may differ from a plain program's by a relative error of at most 0.025.
Values may be sent and summed in bfloat16 or wider, within the bound.
A program may use at most 64 MiB of HBM per device.

v0:
```python
import math

import jax
import jax.numpy as jnp
from jax import lax
from jax.sharding import PartitionSpec as P

HEAD_SIZE = 128
QUERY_HEADS = 32
KEY_VALUE_HEADS = 4


def swapped(value, axis, bit):
    mask = 2**bit
    pairs = [(source, source ^ mask) for source in range(lax.axis_size(axis))]
    return lax.ppermute(value, axis, pairs)


def attend(q4, keys3, values3, grads4, start):
    rows, kv_heads, group_width, width = q4.shape
    scale = 1.0 / math.sqrt(width)
    tile = min(128, rows)
    count = rows // tile
    outputs = []
    query_grads = []
    key_grad = jnp.zeros((rows, kv_heads, width), jnp.float32)
    value_grad = jnp.zeros((rows, kv_heads, width), jnp.float32)
    for block in range(count):
        q_tile = q4[block * tile : (block + 1) * tile]
        g_tile = grads4[block * tile : (block + 1) * tile]
        s_query = start[block * tile : (block + 1) * tile]
        q_place = block * tile + jnp.arange(tile)
        first_position = jnp.sum((start < s_query[0]).astype(jnp.int32)) // tile

        def scores(kt, q_tile=q_tile, s_query=s_query, q_place=q_place):
            k_tile = lax.dynamic_slice_in_dim(keys3, kt * tile, tile, 0)
            v_tile = lax.dynamic_slice_in_dim(values3, kt * tile, tile, 0)
            s_key = lax.dynamic_slice_in_dim(start, kt * tile, tile, 0)
            k_place = kt * tile + jnp.arange(tile)
            visible = (s_query[:, None] == s_key[None, :]) & (k_place[None, :] <= q_place[:, None])
            visible = visible[None, None]
            score = (
                jnp.einsum("qhgd,khd->hgqk", q_tile, k_tile, preferred_element_type=jnp.float32)
                * scale
            )
            return (jnp.where(visible, score, -1e30), visible, k_tile, v_tile)

        def stats_step(kt, carry, scores=scores):
            top, total = carry
            score, visible, k_tile, v_tile = scores(kt)
            new_top = jnp.maximum(top, jnp.max(score, axis=-1))
            expo = jnp.where(visible, jnp.exp(score - new_top[..., None]), 0.0)
            return (new_top, total * jnp.exp(top - new_top) + jnp.sum(expo, axis=-1))

        start_stats = (
            jnp.full((kv_heads, group_width, tile), -1e30, jnp.float32),
            jnp.zeros((kv_heads, group_width, tile), jnp.float32),
        )
        top, total = lax.fori_loop(first_position, block + 1, stats_step, start_stats)

        def probabilities(kt, scores=scores, top=top, total=total):
            score, visible, k_tile, v_tile = scores(kt)
            expo = jnp.where(visible, jnp.exp(score - top[..., None]), 0.0)
            return (expo / total[..., None], k_tile, v_tile)

        def output_step(kt, acc, probabilities=probabilities):
            prob, k_tile, v_tile = probabilities(kt)
            return acc + jnp.einsum(
                "hgqk,khd->qhgd",
                prob.astype(jnp.bfloat16),
                v_tile,
                preferred_element_type=jnp.float32,
            )

        acc = lax.fori_loop(
            first_position,
            block + 1,
            output_step,
            jnp.zeros((tile, kv_heads, group_width, width), jnp.float32),
        )
        out_tile = acc.astype(jnp.bfloat16)
        outputs.append(out_tile)
        delta = jnp.sum(
            g_tile.astype(jnp.float32) * out_tile.astype(jnp.float32), axis=-1
        ).transpose(1, 2, 0)

        def grad_step(
            kt, carry, probabilities=probabilities, delta=delta, q_tile=q_tile, g_tile=g_tile
        ):
            q_acc, k_acc, v_acc = carry
            prob, k_tile, v_tile = probabilities(kt)
            prob_b = prob.astype(jnp.bfloat16)
            dprob = jnp.einsum("qhgd,khd->hgqk", g_tile, v_tile, preferred_element_type=jnp.float32)
            dscore = (prob * (dprob - delta[..., None]) * scale).astype(jnp.bfloat16)
            q_acc = q_acc + jnp.einsum(
                "hgqk,khd->qhgd", dscore, k_tile, preferred_element_type=jnp.float32
            )
            k_part = jnp.einsum(
                "hgqk,qhgd->khd", dscore, q_tile, preferred_element_type=jnp.float32
            )
            v_part = jnp.einsum(
                "hgqk,qhgd->khd", prob_b, g_tile, preferred_element_type=jnp.float32
            )
            k_old = lax.dynamic_slice_in_dim(k_acc, kt * tile, tile, 0)
            v_old = lax.dynamic_slice_in_dim(v_acc, kt * tile, tile, 0)
            k_acc = lax.dynamic_update_slice_in_dim(k_acc, k_old + k_part, kt * tile, 0)
            v_acc = lax.dynamic_update_slice_in_dim(v_acc, v_old + v_part, kt * tile, 0)
            return (q_acc, k_acc, v_acc)

        q_acc, key_grad, value_grad = lax.fori_loop(
            first_position,
            block + 1,
            grad_step,
            (jnp.zeros((tile, kv_heads, group_width, width), jnp.float32), key_grad, value_grad),
        )
        query_grads.append(q_acc.astype(jnp.bfloat16))
    return (jnp.concatenate(outputs, 0), jnp.concatenate(query_grads, 0), key_grad, value_grad)


def on_device(queries, keys, values, output_gradient, doc_start):
    rows = queries.shape[0]
    kv_heads = keys.shape[1] // HEAD_SIZE
    group_width = QUERY_HEADS // KEY_VALUE_HEADS
    q4 = queries.reshape(rows, kv_heads, group_width, HEAD_SIZE)
    g4 = output_gradient.reshape(rows, kv_heads, group_width, HEAD_SIZE)
    k3 = keys.reshape(rows, kv_heads, HEAD_SIZE)
    v3 = values.reshape(rows, kv_heads, HEAD_SIZE)
    partner_bit = lax.axis_size("ctx").bit_length() - 2
    half = group_width // 2
    lent = swapped(
        (jnp.stack((q4[:, :, half:], g4[:, :, half:])), jnp.stack((k3, v3)), doc_start),
        "ctx",
        partner_bit,
    )
    own = attend(q4[:, :, :half], k3, v3, g4[:, :, :half], doc_start)
    guest = attend(lent[0][0], lent[1][0], lent[1][1], lent[0][1], lent[2])
    back_rows = swapped(jnp.stack((guest[0], guest[1])), "ctx", partner_bit)
    back_sums = swapped(jnp.stack((guest[2], guest[3])), "ctx", partner_bit)
    out4 = jnp.concatenate((own[0], back_rows[0]), 2)
    dq4 = jnp.concatenate((own[1], back_rows[1]), 2)
    key_grad = own[2] + back_sums[0]
    value_grad = own[3] + back_sums[1]
    attended = lax.all_to_all(
        out4.reshape(rows, kv_heads * group_width * HEAD_SIZE),
        "tp",
        split_axis=0,
        concat_axis=1,
        tiled=True,
    )
    return (
        attended,
        dq4.reshape(rows, kv_heads * group_width * HEAD_SIZE),
        key_grad.astype(jnp.bfloat16).reshape(rows, kv_heads * HEAD_SIZE),
        value_grad.astype(jnp.bfloat16).reshape(rows, kv_heads * HEAD_SIZE),
    )


def solution(mesh):
    return jax.shard_map(
        on_device,
        mesh=mesh,
        in_specs=(P("ctx", "tp"), P("ctx", "tp"), P("ctx", "tp"), P("ctx", "tp"), P("ctx")),
        out_specs=(P(("ctx", "tp"), None), P("ctx", "tp"), P("ctx", "tp"), P("ctx", "tp")),
        check_vma=False,
    )
```

profile of v0, /device:TPU:32, one launch (start us, length us, event | category | flops | bytes accessed | tf_op | source)
XLA Modules:
  0.0 250.2 jit_solution(16746920482975794205)
XLA Ops:
  0.6 10.9 %collective-permute-start = (s32[512]{0:T(512)}, s32[512]{0:T(512)}, u32[]{:S(2)}, u32[]{:S(2)}) collective-permute-start(s32[512]{0:T(512)} %param.57), channel_id=1, source_target_pairs={{0,256},{4,260},{8,264},{12,268},{16,272},{20,276},{24,280},{28,28... | collective-permute-start | bytes 6152 | tf_op jit(solution)/shard_map/ppermute | solution.py:16
  11.6 1.5 copy.169
  13.1 1.5 copy.182
  15.7 1.9 collective-permute-start.2
  18.4 7.8 %collective-permute-start.1 = (bf16[2,512,1,128]{3,1,2,0:T(8,128)(2,1)}, bf16[2,512,1,128]{3,1,2,0:T(8,128)(2,1)}, u32[]{:S(2)}, u32[]{:S(2)}) collective-permute-start(bf16[2,512,1,128]{3,1,2,0:T(8,128)(2,1)} %pad_maximum_fusion.5), channel_id=1, source_target_pairs={{0,256},{4,260},{8,264},{12,268},{16,272},{20,276},{24,280},{28,28... | collective-permute-start | bytes 786440 | tf_op jit(solution)/shard_map/ppermute | solution.py:16
  26.8 3.2 %convert_reduce_fusion.7 = (s32[]{:T(128)}, s32[]{:T(128)}, s32[]{:T(128)}, s32[]{:T(128)}) fusion(s32[512]{0:T(512)S(1)} %copy-done.48, s32[]{:T(128)} %bitcast, s32[]{:T(128)} %bitcast.6, s32[]{:T(128)} %bitcast.5, s32[]{:T(128)} %bitcast.4), kind=kLoop, calls=%fused_computation.717 | loop fusion | flops 6140 | bytes 2080 | tf_op jit(solution)/shard_map/reduce_sum | solution.py:33
  43.7 1.3 while.315
  45.6 1.6 while.316
  47.3 4.2 %while.317 = (s32[]{:T(128)}, f32[128,1,4,128]{0,3,2,1:T(8,128)S(1)}, bf16[512,1,128]{0,2,1:T(8,128)(2,1)}, s32[128]{0:T(128)S(1)}, s32[512]{0:T(512)S(1)}, /*in...) while((s32[]{:T(128)}, ...), condition=%wide.region_20.21_spmd.clone, body=%wide.region_19.20_spmd.clone.sunk | while | flops 34062596 | bytes 763059 | solution.py:75
  47.5 1.2 fusion.792
  48.9 1.2 fusion.792
  52.0 2.1 while.318
  54.2 5.5 %while.319 = (s32[]{:T(128)}, f32[128,1,4,128]{0,3,2,1:T(8,128)S(1)}, bf16[512,1,128]{0,2,1:T(8,128)(2,1)}, s32[128]{0:T(128)S(1)}, s32[512]{0:T(512)S(1)}, /*in...) while((s32[]{:T(128)}, ...), condition=%wide.region_27.28_spmd.clone, body=%wide.region_26.27_spmd.clone.sunk | while | flops 34062596 | bytes 763059 | solution.py:75
  61.0 1.5 multiply_reduce_fusion
  62.6 1.3 while.332
  64.0 2.5 %while.333 = (s32[]{:T(128)}, f32[128,1,4,128]{0,3,2,1:T(8,128)S(1)}, f32[512,1,128]{2,0,1:T(8,128)S(1)}, f32[512,1,128]{2,0,1:T(8,128)S(1)}, bf16[512,1,128]{2,...) while((s32[]{:T(128)}, ...), condition=%wide.region_73.74_spmd.clone, body=%wide.region_72.73_spmd.clone.sunk | while | flops 84689152 | bytes 2631911 | solution.py:110
  66.7 1.4 fusion.593
  68.1 4.0 %convert_reduce_fusion.3 = (s32[]{:T(128)}, s32[]{:T(128)}, s32[]{:T(128)}, s32[]{:T(128)}) fusion(s32[512]{0:T(512)} %collective-permute-done, s32[]{:T(128)} %bitcast.7, s32[]{:T(128)} %bitcast.20, s32[]{:T(128)} %bitcast.18, s32[]{:T(128)} %bitcast.16), kind=kLoop, calls=%fused_computation.713 | loop fusion | flops 6140 | bytes 2080 | tf_op jit(solution)/shard_map/reduce_sum | solution.py:33
  81.8 1.4 fusion.592
  84.4 2.1 slice_bitcast_fusion.6
  86.7 2.4 while.326
  89.1 2.6 %while.327 = (s32[]{:T(128)}, f32[128,1,4,128]{0,3,2,1:T(8,128)S(1)}, bf16[512,1,128]{0,2,1:T(8,128)(2,1)S(1)}, s32[128]{0:T(128)S(1)}, s32[512]{0:T(512)}, /*in...) while((s32[]{:T(128)}, ...), condition=%wide.region_55.56_spmd.clone, body=%wide.region_54.55_spmd.clone.sunk | while | flops 34062596 | bytes 763059 | solution.py:75
  93.0 2.4 while.324
  95.4 4.1 %while.325 = (s32[]{:T(128)}, f32[128,1,4,128]{0,3,2,1:T(8,128)S(1)}, bf16[512,1,128]{0,2,1:T(8,128)(2,1)}, s32[128]{0:T(128)S(1)}, s32[512]{0:T(512)}, /*index=...) while((s32[]{:T(128)}, ...), condition=%wide.region_48.49_spmd.clone, body=%wide.region_47.48_spmd.clone.sunk | while | flops 34062596 | bytes 763059 | solution.py:75
  101.3 2.4 while.322
  103.8 4.1 %while.323 = (s32[]{:T(128)}, f32[128,1,4,128]{0,3,2,1:T(8,128)S(1)}, bf16[512,1,128]{0,2,1:T(8,128)(2,1)}, s32[128]{0:T(128)S(1)}, s32[512]{0:T(512)}, /*index=...) while((s32[]{:T(128)}, ...), condition=%wide.region_41.42_spmd.clone, body=%wide.region_40.41_spmd.clone.sunk | while | flops 34062596 | bytes 763059 | solution.py:75
  109.2 1.2 while.320
  111.1 3.7 %while.321 = (s32[]{:T(128)}, f32[128,1,4,128]{0,3,2,1:T(8,128)}, bf16[512,1,128]{0,2,1:T(8,128)(2,1)}, s32[128]{0:T(128)}, s32[512]{0:T(512)}, /*index=5*/bf16[...) while((s32[]{:T(128)}, f32[128,1,4,128]{0,3,2,1:T(8,128)}, ...), condition=%wide.region_34.35_spmd.clone, body=%wide.region_33.34_spmd.clone.sunk | while | flops 34062468 | bytes 762035 | solution.py:75
  112.7 2.1 fusion.804
  115.5 2.7 %multiply_reduce_fusion.4 = (f32[128,4]{0,1:T(4,128)}, f32[128,4]{0,1:T(4,128)}, f32[128,4]{0,1:T(4,128)}, f32[128,4]{0,1:T(4,128)S(1)}, bf16[128,1,4,128]{0,3,2...) fusion(bf16[2,512,1,4,128]{1,4,3,2,0:T(8,128)(2,1)} %collective, ...), kind=kLoop, calls=%fused_computation.694 | loop fusion | flops 1308672 | bytes 2105344 | tf_op jit(solution)/shard_map/reduce_sum | solution.py:83
  118.3 1.9 while.328
  121.3 6.6 %while.329 = (s32[]{:T(128)}, f32[128,1,4,128]{0,3,2,1:T(8,128)S(1)}, f32[512,1,128]{2,0,1:T(8,128)S(1)}, f32[512,1,128]{2,0,1:T(8,128)S(1)}, bf16[512,1,128]{2,...) while((s32[]{:T(128)}, ...), condition=%wide.region_61.62_spmd.clone, body=%wide.region_60.61_spmd.clone.sunk | while | flops 84689152 | bytes 2640131 | solution.py:110
  129.1 8.0 %while.330 = (s32[]{:T(128)}, f32[128,1,4,128]{0,3,2,1:T(8,128)S(1)}, f32[512,1,128]{2,0,1:T(8,128)S(1)}, f32[512,1,128]{2,0,1:T(8,128)S(1)}, bf16[512,1,128]{2,...) while((s32[]{:T(128)}, ...), condition=%wide.region_64.65_spmd.clone, body=%wide.region_63.64_spmd.clone.sunk | while | flops 84689152 | bytes 2640131 | solution.py:110
  138.3 11.2 %while.331 = (s32[]{:T(128)}, f32[128,1,4,128]{0,3,2,1:T(8,128)S(1)}, f32[512,1,128]{2,0,1:T(8,128)}, f32[512,1,128]{2,0,1:T(8,128)S(1)}, bf16[512,1,128]{2,0,1:...) while((s32[]{:T(128)}, ...), condition=%wide.region_67.68_spmd.clone, body=%wide.region_66.67_spmd.clone.sunk | while | flops 84689152 | bytes 2640131 | solution.py:110
  141.7 1.7 fusion.879
  147.2 1.7 fusion.879
  151.8 19.4 %collective-permute-start.3 = (bf16[2,512,1,4,128]{1,4,3,2,0:T(8,128)(2,1)}, bf16[2,512,1,4,128]{1,4,3,2,0:T(8,128)(2,1)}, u32[]{:S(2)}, u32[]{:S(2)}) collective-permute-start(bf16[2,512,1,4,128]{1,4,3,2,0:T(8,128)(2,1)} %pad_maximum_fusion.1), channel_id=1, source_target_pairs={{0,256},{4,260},{8,264},{12,268},{16,272},{20,276},{24,280},{28,28... | collective-permute-start | bytes 3145736 | tf_op jit(solution)/shard_map/ppermute | solution.py:16
  171.3 3.8 %while.334 = (s32[]{:T(128)}, f32[128,1,4,128]{0,3,2,1:T(8,128)S(1)}, f32[512,1,128]{2,0,1:T(8,128)S(1)}, f32[512,1,128]{2,0,1:T(8,128)S(1)}, bf16[512,1,128]{2,...) while((s32[]{:T(128)}, ...), condition=%wide.region_76.77_spmd.clone, body=%wide.region_75.76_spmd.clone.sunk | while | flops 84689152 | bytes 2631911 | solution.py:110
  176.1 2.1 collective-permute-start.4
  178.1 44.4 %collective-permute-done.3 = bf16[2,512,1,4,128]{1,4,3,2,0:T(8,128)(2,1)} collective-permute-done((bf16[2,512,1,4,128]{1,4,3,2,0:T(8,128)(2,1)}, bf16[2,512,1,4,128]{1,4,3,2,0:T(8,128)(2,1)}, u32[]{:S(2)}, u32[]{:S(2)}) %collective-permute-start.3) | collective-permute-done | bytes 1048608 | tf_op jit(solution)/shard_map/ppermute | solution.py:16
  222.6 2.1 slice_bitcast_fusion
  225.9 2.4 copy.239
  228.3 4.3 %all-to-all-start = ((bf16[4,128,1024]{2,1,0:T(8,128)(2,1)}), bf16[4,128,1024]{2,1,0:T(8,128)(2,1)S(1)}, u32[]{:S(2)}, u32[]{:S(2)}) async-start(bf16[4,128,1024]{2,1,0:T(8,128)(2,1)} %copy.239), calls=%async_computation | async-start | bytes 2097152 | tf_op jit(solution)/shard_map/all_to_all | solution.py:143
  232.6 5.0 %while.335 = (s32[]{:T(128)}, f32[128,1,4,128]{0,3,2,1:T(8,128)S(1)}, f32[512,1,128]{2,0,1:T(8,128)S(1)}, f32[512,1,128]{2,0,1:T(8,128)S(1)}, bf16[512,1,128]{2,...) while((s32[]{:T(128)}, ...), condition=%wide.region_79.80_spmd.clone, body=%wide.region_78.79_spmd.clone.sunk | while | flops 84689152 | bytes 2631911 | solution.py:110
  237.8 1.8 fusion.579
  239.7 1.3 copy.240
  241.0 7.1 %all-to-all-done = bf16[4,128,1024]{2,1,0:T(8,128)(2,1)S(1)} async-done(((bf16[4,128,1024]{2,1,0:T(8,128)(2,1)}), bf16[4,128,1024]{2,1,0:T(8,128)(2,1)S(1)}, u32[]{:S(2)}, u32[]{:S(2)}) %all-to-all-start) | async-done | bytes 1048608 | tf_op jit(solution)/shard_map/all_to_all | solution.py:143
  248.8 1.3 copy.214
  (528 shorter events, 94.0 us)
Async XLA Ops:
  0.6 66.1 %collective-permute-start = (s32[512]{0:T(512)}, s32[512]{0:T(512)}, u32[]{:S(2)}, u32[]{:S(2)}) collective-permute-start(s32[512]{0:T(512)} %param.57), channel_id=1, source_target_pairs={{0,256},{4,260},{8,264},{12,268},{16,272},{20,276},{24,280},{28,28... | collective-permute-start | bytes 6152 | tf_op jit(solution)/shard_map/ppermute | solution.py:16
  14.6 3.0 %copy-start = (bf16[512,128]{1,0:T(8,128)(2,1)S(1)}, bf16[512,128]{1,0:T(8,128)(2,1)}, u32[]{:S(2)}) copy-start(bf16[512,128]{1,0:T(8,128)(2,1)} %param.54) | copy-start | bytes 393220
  14.7 3.0 %copy-start.3 = (bf16[512,128]{1,0:T(8,128)(2,1)S(1)}, bf16[512,128]{1,0:T(8,128)(2,1)}, u32[]{:S(2)}) copy-start(bf16[512,128]{1,0:T(8,128)(2,1)} %param.55) | copy-start | bytes 393220
  14.7 11.6 %copy-start.48 = (s32[512]{0:T(512)S(1)}, s32[512]{0:T(512)}, u32[]{:S(2)}) copy-start(s32[512]{0:T(512)} %param.57) | copy-start | bytes 6148
  15.7 68.6 %collective-permute-start.2 = (bf16[2,512,1,4,128]{1,4,3,2,0:T(8,128)(2,1)}, bf16[2,512,1,4,128]{1,4,3,2,0:T(8,128)(2,1)}, u32[]{:S(2)}, u32[]{:S(2)}) collective-permute-start(bf16[2,512,1,4,128]{1,4,3,2,0:T(8,128)(2,1)} %pad_maximum_fusion), channel_id=1, source_target_pairs={{0,256},{4,260},{8,264},{12,268},{16,272},{20,276},{24,280},{28,28... | collective-permute-start | bytes 3145736 | tf_op jit(solution)/shard_map/ppermute | solution.py:16
  18.4 64.8 %collective-permute-start.1 = (bf16[2,512,1,128]{3,1,2,0:T(8,128)(2,1)}, bf16[2,512,1,128]{3,1,2,0:T(8,128)(2,1)}, u32[]{:S(2)}, u32[]{:S(2)}) collective-permute-start(bf16[2,512,1,128]{3,1,2,0:T(8,128)(2,1)} %pad_maximum_fusion.5), channel_id=1, source_target_pairs={{0,256},{4,260},{8,264},{12,268},{16,272},{20,276},{24,280},{28,28... | collective-permute-start | bytes 786440 | tf_op jit(solution)/shard_map/ppermute | solution.py:16
  66.5 16.7 %copy-start.49 = (s32[512]{0:T(512)}, s32[512]{0:T(512)S(1)}, u32[]{:S(2)}) copy-start(s32[512]{0:T(512)S(1)} %get-tuple-element.5795) | copy-start | bytes 6148
  100.6 0.7 copy-start.6
  100.6 0.7 copy-start.20
  103.8 4.9 %copy-start.30 = (s32[128]{0:T(128)S(1)}, s32[128]{0:T(128)}, u32[]{:S(2)}) copy-start(s32[128]{0:T(128)} %get-tuple-element.5009) | copy-start | bytes 1540
  108.5 0.7 copy-start.8
  108.5 0.7 copy-start.22
  108.5 0.7 copy-start.40
  111.1 4.2 %copy-start.14 = (bf16[128,1,4,128]{0,3,2,1:T(8,128)(2,1)S(1)}, bf16[128,1,4,128]{0,3,2,1:T(8,128)(2,1)}, u32[]{:S(2)}) copy-start(bf16[128,1,4,128]{0,3,2,1:T(8,128)(2,1)} %get-tuple-element.3169) | copy-start | bytes 393220
  111.1 4.4 %copy-start.7 = (f32[128,1,4,128]{0,3,2,1:T(8,128)S(1)}, f32[128,1,4,128]{0,3,2,1:T(8,128)}, u32[]{:S(2)}) copy-start(f32[128,1,4,128]{0,3,2,1:T(8,128)} %copy-done.6) | copy-start | bytes 786436
  111.1 4.4 %copy-start.9 = (f32[128,1,4,128]{0,3,2,1:T(8,128)S(1)}, f32[128,1,4,128]{0,3,2,1:T(8,128)}, u32[]{:S(2)}) copy-start(f32[128,1,4,128]{0,3,2,1:T(8,128)} %copy-done.8) | copy-start | bytes 786436
  115.5 2.8 %copy-start.31 = (s32[128]{0:T(128)S(1)}, s32[128]{0:T(128)}, u32[]{:S(2)}) copy-start(s32[128]{0:T(128)} %get-tuple-element.5770) | copy-start | bytes 1540
  115.5 2.8 %copy-start.42 = (f32[1,4,128]{2,1,0:T(4,128)S(1)}, f32[1,4,128]{2,1,0:T(4,128)}, u32[]{:S(2)}) copy-start(f32[1,4,128]{2,1,0:T(4,128)} %copy-done.41) | copy-start | bytes 6148
  121.3 7.8 %copy-start.21 = (f32[1,4,128]{2,1,0:T(4,128)S(1)}, f32[1,4,128]{2,1,0:T(4,128)}, u32[]{:S(2)}) copy-start(f32[1,4,128]{2,1,0:T(4,128)} %copy-done.20) | copy-start | bytes 6148
  121.4 2.5 copy-start.47
  124.7 2.5 copy-start.47
  128.0 1.1 copy-start.4
  129.1 2.4 copy-start.46
  133.1 2.4 copy-start.46
  137.1 1.1 copy-start.1
  138.3 2.4 copy-start.45
  143.8 2.4 copy-start.45
  149.4 0.9 copy-start.15
  149.5 1.0 copy-start.16
  149.5 1.0 copy-start.17
  149.5 1.1 copy-start.18
  150.7 20.6 %copy-start.26 = (s32[128]{0:T(128)S(1)}, s32[128]{0:T(128)}, u32[]{:S(2)}) copy-start(s32[128]{0:T(128)} %copy-done.25) | copy-start | bytes 1540
  150.7 20.6 %copy-start.35 = (f32[1,4,128]{2,1,0:T(4,128)S(1)}, f32[1,4,128]{2,1,0:T(4,128)}, u32[]{:S(2)}) copy-start(f32[1,4,128]{2,1,0:T(4,128)} %copy-done.34) | copy-start | bytes 6148
  150.7 20.6 %copy-start.44 = (f32[128,4]{0,1:T(4,128)S(1)}, f32[128,4]{0,1:T(4,128)}, u32[]{:S(2)}) copy-start(f32[128,4]{0,1:T(4,128)} %get-tuple-element.2619) | copy-start | bytes 6148
  150.7 20.6 %copy-start.50 = (s32[512]{0:T(512)S(1)}, s32[512]{0:T(512)}, u32[]{:S(2)}) copy-start(s32[512]{0:T(512)} %copy-done.49) | copy-start | bytes 6148
  151.8 70.8 %collective-permute-start.3 = (bf16[2,512,1,4,128]{1,4,3,2,0:T(8,128)(2,1)}, bf16[2,512,1,4,128]{1,4,3,2,0:T(8,128)(2,1)}, u32[]{:S(2)}, u32[]{:S(2)}) collective-permute-start(bf16[2,512,1,4,128]{1,4,3,2,0:T(8,128)(2,1)} %pad_maximum_fusion.1), channel_id=1, source_target_pairs={{0,256},{4,260},{8,264},{12,268},{16,272},{20,276},{24,280},{28,28... | collective-permute-start | bytes 3145736 | tf_op jit(solution)/shard_map/ppermute | solution.py:16
  171.3 3.8 %copy-start.19 = (bf16[128,1,4,128]{0,3,2,1:T(8,128)(2,1)S(1)}, bf16[128,1,4,128]{0,3,2,1:T(8,128)(2,1)}, u32[]{:S(2)}) copy-start(bf16[128,1,4,128]{0,3,2,1:T(8,128)(2,1)} %get-tuple-element.3156) | copy-start | bytes 393220
  171.3 3.9 %copy-start.2 = (f32[512,1,128]{2,0,1:T(8,128)S(1)}, f32[512,1,128]{2,0,1:T(8,128)}, u32[]{:S(2)}) copy-start(f32[512,1,128]{2,0,1:T(8,128)} %get-tuple-element.1401) | copy-start | bytes 786436
  176.1 48.6 %copy-start.10 = (bf16[128,1,4,128]{0,3,2,1:T(8,128)(2,1)S(1)}, bf16[128,1,4,128]{0,3,2,1:T(8,128)(2,1)}, u32[]{:S(2)}) copy-start(bf16[128,1,4,128]{0,3,2,1:T(8,128)(2,1)} %get-tuple-element.3096) | copy-start | bytes 393220
  176.1 48.6 %copy-start.11 = (bf16[128,1,4,128]{0,3,2,1:T(8,128)(2,1)S(1)}, bf16[128,1,4,128]{0,3,2,1:T(8,128)(2,1)}, u32[]{:S(2)}) copy-start(bf16[128,1,4,128]{0,3,2,1:T(8,128)(2,1)} %get-tuple-element.3097) | copy-start | bytes 393220
  176.1 48.6 %copy-start.12 = (bf16[128,1,4,128]{0,3,2,1:T(8,128)(2,1)S(1)}, bf16[128,1,4,128]{0,3,2,1:T(8,128)(2,1)}, u32[]{:S(2)}) copy-start(bf16[128,1,4,128]{0,3,2,1:T(8,128)(2,1)} %get-tuple-element.3098) | copy-start | bytes 393220
  176.1 48.6 %copy-start.13 = (bf16[128,1,4,128]{0,3,2,1:T(8,128)(2,1)S(1)}, bf16[128,1,4,128]{0,3,2,1:T(8,128)(2,1)}, u32[]{:S(2)}) copy-start(bf16[128,1,4,128]{0,3,2,1:T(8,128)(2,1)} %get-tuple-element.3099) | copy-start | bytes 393220
  176.1 61.7 %collective-permute-start.4 = (f32[2,512,1,128]{3,1,2,0:T(8,128)}, f32[2,512,1,128]{3,1,2,0:T(8,128)}, u32[]{:S(2)}, u32[]{:S(2)}) collective-permute-start(f32[2,512,1,128]{3,1,2,0:T(8,128)} %pad_maximum_fusion.4), channel_id=1, source_target_pairs={{0,256},{4,260},{8,264},{12,268},{16,272},{20,276},{24,280},{28,28... | collective-permute-start | bytes 1572872 | tf_op jit(solution)/shard_map/ppermute | solution.py:16
  228.3 4.3 %copy-start.24 = (s32[128]{0:T(128)S(1)}, s32[128]{0:T(128)}, u32[]{:S(2)}) copy-start(s32[128]{0:T(128)} %copy-done.23) | copy-start | bytes 1540
  228.3 4.3 %copy-start.37 = (f32[1,4,128]{2,1,0:T(4,128)S(1)}, f32[1,4,128]{2,1,0:T(4,128)}, u32[]{:S(2)}) copy-start(f32[1,4,128]{2,1,0:T(4,128)} %copy-done.36) | copy-start | bytes 6148
  228.3 4.3 %copy-start.43 = (f32[128,4]{0,1:T(4,128)S(1)}, f32[128,4]{0,1:T(4,128)}, u32[]{:S(2)}) copy-start(f32[128,4]{0,1:T(4,128)} %get-tuple-element.2616) | copy-start | bytes 6148
  228.3 19.9 %all-to-all-start = ((bf16[4,128,1024]{2,1,0:T(8,128)(2,1)}), bf16[4,128,1024]{2,1,0:T(8,128)(2,1)S(1)}, u32[]{:S(2)}, u32[]{:S(2)}) async-start(bf16[4,128,1024]{2,1,0:T(8,128)(2,1)} %copy.239), calls=%async_computation | async-start | bytes 2097152 | tf_op jit(solution)/shard_map/all_to_all | solution.py:143
  237.7 1.9 copy-start.5
  (12 other events, 7.0 us)
where the time goes:
time: 254 us; the launch traced here: 250 us
  waiting for transfers between devices  51.6 us (20%)
  local copies, waits for them, and re-layouts  51.4 us (20%)
  matrix products  47.6 us (19%)
  starting transfers between devices  46.4 us (18%)
  other arithmetic  28.8 us (11%)
  between operations  21.5 us (8%)
  loops' own time  2.9 us (1%)
    ppermute x5, waiting for transfers between devices, swapped(): return lax.ppermute(value, axis, pairs)  44.4 us
    ppermute x5, starting transfers between devices, swapped(): return lax.ppermute(value, axis, pairs)  42.1 us
    dynamic_slice x51, local copies, waits for them, and re-layouts, scores(): s_key = lax.dynamic_slice_in_dim(start, kt * tile, tile, 0)  18.1 us
    unnamed x117, local copies, waits for them, and re-layouts  17 us
    dot_general x17, matrix products, output_step(): jnp.einsum('hgqk,khd->qhgd', prob.astype(jnp.bfloat16), v_tile, preferred...  16.9 us
    dot_general x34, matrix products, scores(): jnp.einsum('qhgd,khd->hgqk', q_tile, k_tile, preferred_element_type=jnp.f...  11.5 us
    and x51, other arithmetic, scores(): (s_query[:, None] == s_key[None, :]) & (k_place[None, :] <= q_place[:, No...  9.71 us
    reduce_sum x2, other arithmetic, attend(): first_position = jnp.sum((start < s_query[0]).astype(jnp.int32)) // tile  7.21 us
  transfers between devices with their start and end apart: 6, of which 2 were waited for; matrix products, arithmetic and copies ran while one was open for 23% of the time, Pallas kernels for 0%

commit v1 on v0

v1 whole, which is shorter than its diff:
```python
import functools
import math

import jax
import jax.numpy as jnp
from jax import lax
from jax.experimental import pallas as pl
from jax.experimental.pallas import tpu as pltpu
from jax.sharding import PartitionSpec as P

MESH = pl.DeviceIdType.MESH
BF, F32 = jnp.bfloat16, jnp.float32
NT = (((1,), (1,)), ((), ()))
NN = (((1,), (0,)), ((), ()))
HEAD = 128
TILE = 128
HEADS = 8
ROWS = 512
BLOCKS = 4
SCALE = 1.0 / math.sqrt(HEAD)
SCALE2 = math.log2(math.e) / math.sqrt(HEAD)
FIRST = (0, 128, 384, 768)
STACKED = 1280
ORDER = (2, 1, 3, 0)
BARRIER_AFTER = 1
WIDTH = 4
PIECES = 1
VM2 = 2**20
GROUPS = HEADS // WIDTH


def head_cols(first, count=1):
    return pl.ds(pl.multiple_of(first * HEAD, HEAD), count * HEAD)


def stacked(ref, t, p):
    rows = slice(TILE * t, TILE * (t + 1))
    return [ref[rows, head_cols(p * WIDTH + x)] for x in range(WIDTH)]


def prepare(t, base, start, k, kaug):
    n, o = TILE * (t + 1), FIRST[t]
    kaug[o : o + n, 0:HEAD] = k[0:n, :]
    first = (start[pl.ds(TILE * t, TILE)] - base)[None, :]
    j = lax.broadcasted_iota(jnp.int32, (n, TILE), 0)
    i = lax.broadcasted_iota(jnp.int32, (n, TILE), 1) + TILE * t
    kaug[o : o + n, HEAD : 2 * HEAD] = jnp.where((j >= first) & (j <= i), 0.0, -1e30).astype(BF)


def forward(t, p, q, kaug, vt, prob, out):
    n, o = TILE * (t + 1), FIRST[t]
    eye = lax.broadcasted_iota(jnp.int32, (TILE, TILE), 0) == lax.broadcasted_iota(
        jnp.int32, (TILE, TILE), 1
    )
    eye = eye.astype(F32).astype(BF)
    queries = jnp.concatenate([jnp.concatenate([x, eye], 1) for x in stacked(q, t, p)], 0)
    score = lax.dot_general(kaug[o : o + n, :], queries, NT, preferred_element_type=F32)
    top = jnp.max(score, axis=0, keepdims=True)
    expo = jnp.exp2((score - top) * SCALE2)
    prob_b = (expo * (1.0 / jnp.sum(expo, axis=0, keepdims=True))).astype(BF)
    prob[p, o : o + n, :] = prob_b
    out_t = lax.dot_general(vt[:, 0:n], prob_b, NN, preferred_element_type=F32)
    for x in range(WIDTH):
        out[TILE * t : TILE * (t + 1), head_cols(p * WIDTH + x)] = out_t[
            :, HEAD * x : HEAD * (x + 1)
        ].T.astype(BF)


def backward(t, p, q, g, v, kt, prob, dq, dk, dv):
    n, o = TILE * (t + 1), FIRST[t]
    queries = jnp.concatenate(stacked(q, t, p), 0)
    grads = jnp.concatenate(stacked(g, t, p), 0)
    prob_b = prob[p, o : o + n, :]
    dprob = lax.dot_general(v[0:n, :], grads, NT, preferred_element_type=F32)
    prob_f = prob_b.astype(F32)
    delta = jnp.sum(prob_f * dprob, axis=0, keepdims=True)
    dscore = (prob_f * (dprob - delta)).astype(BF)
    dq_t = lax.dot_general(kt[:, 0:n], dscore, NN, preferred_element_type=F32) * SCALE
    for x in range(WIDTH):
        dq[TILE * t : TILE * (t + 1), head_cols(p * WIDTH + x)] = dq_t[
            :, HEAD * x : HEAD * (x + 1)
        ].T.astype(BF)
    dk[0:n, :] += lax.dot_general(dscore, queries, NN, preferred_element_type=F32)
    dv[0:n, :] += lax.dot_general(prob_b, grads, NN, preferred_element_type=F32)


def groups(body):
    def step(p, carry):
        body(p)
        return carry

    lax.fori_loop(0, GROUPS, step, 0)


def kernel(
    q_in, k_in, v_in, g_in, start_in,
    att_out, dq_out, dk_out, dv_out,
    q, k, v, g, start, kaug, kt, vt, prob, out, dq, dk, dv, dk_b, dv_b,
    q_sem, g_sem, kv_sem, send_sem, recv_sem, own_sem, dq_sem, kv_out_sem,
):
    me = lax.axis_index("tp")
    base = lax.axis_index("ctx") * ROWS
    peers = [lax.rem(me + off, BLOCKS) for off in ORDER]
    barrier = pltpu.get_barrier_semaphore()
    for peer in peers[:3]:
        pl.semaphore_signal(barrier, inc=1, device_id={"tp": peer}, device_id_type=MESH)

    loads = [
        pltpu.make_async_copy(src, dst, kv_sem.at[i])
        for i, (src, dst) in enumerate(((k_in, k), (start_in, start), (v_in, v)))
    ]
    for copy in loads:
        copy.start()

    def block(ref, t):
        return ref.at[pl.ds(pl.multiple_of(t * TILE, TILE), TILE)]

    def load(src, dst, sems):
        copies = []
        for i, peer in enumerate(peers):
            copies.append(pltpu.make_async_copy(block(src, peer), block(dst, peer), sems.at[i]))
            copies[-1].start()
        return copies

    q_loads = load(q_in, q, q_sem)
    g_loads = load(g_in, g, g_sem)
    for copy in loads:
        copy.wait()
    vt[...] = v[...].T

    mine = pl.ds(pl.multiple_of(me * HEADS * HEAD, HEADS * HEAD), HEADS * HEAD)
    sends = []

    def send(i):
        sends.append(
            pltpu.make_async_remote_copy(
                src_ref=block(out, peers[i]),
                dst_ref=att_out.at[:, mine],
                send_sem=send_sem.at[i],
                recv_sem=recv_sem.at[i],
                device_id={"tp": peers[i]},
                device_id_type=MESH,
            )
        )
        sends[-1].start()

    for i, peer in enumerate(peers):
        q_loads[i].wait()

        def one(t):
            prepare(t, base, start, k, kaug)
            groups(lambda p: forward(t, p, q, kaug, vt, prob, out))

        lax.switch(peer, [functools.partial(one, t) for t in range(BLOCKS)])
        if i == BARRIER_AFTER:
            pl.semaphore_wait(barrier, 3)
            for early in range(i + 1):
                send(early)
        elif i > BARRIER_AFTER and i < 3:
            send(i)
    own = pltpu.make_async_copy(block(out, me), att_out.at[:, mine], own_sem)
    own.start()

    kt[...] = k[...].T
    dk[...] = jnp.zeros_like(dk)
    dv[...] = jnp.zeros_like(dv)
    for copy in g_loads:
        copy.wait()
    stores = []
    for t in range(BLOCKS):
        groups(lambda p, t=t: backward(t, p, q, g, v, kt, prob, dq, dk, dv))
        stores.append(
            pltpu.make_async_copy(
                dq.at[pl.ds(TILE * t, TILE)], dq_out.at[pl.ds(TILE * t, TILE)], dq_sem.at[t]
            )
        )
        stores[-1].start()
    dk_b[...] = (dk[...] * SCALE).astype(BF)
    dv_b[...] = dv[...].astype(BF)
    for i, (src, dst) in enumerate(((dk_b, dk_out), (dv_b, dv_out))):
        stores.append(pltpu.make_async_copy(src, dst, kv_out_sem.at[i]))
        stores[-1].start()
    for copy in stores:
        copy.wait()
    own.wait()
    for copy in sends:
        copy.wait()


def deliver(*refs):
    sems = refs[8]
    copies = []
    for i in range(4):
        rows = refs[i].shape[0]
        pieces = PIECES if i < 2 else 1
        for c in range(pieces):
            part = pl.ds(c * (rows // pieces), rows // pieces)
            copies.append(
                pltpu.make_async_copy(refs[i].at[part], refs[4 + i].at[part], sems.at[i, c])
            )
            copies[-1].start()
    for copy in copies:
        copy.wait()


def on_device(queries, keys, values, output_gradient, doc_start):
    anywhere = pl.BlockSpec(memory_space=pl.ANY)
    hbm = pl.BlockSpec(memory_space=pltpu.HBM)
    dma = pltpu.SemaphoreType.DMA
    queries, keys, values, output_gradient, doc_start = (
        pltpu.with_memory_space_constraint(x, pltpu.HBM)
        for x in (queries, keys, values, output_gradient, doc_start)
    )
    results = pl.pallas_call(
        kernel,
        out_shape=(
            jax.ShapeDtypeStruct((TILE, BLOCKS * HEADS * HEAD), BF),
            jax.ShapeDtypeStruct((ROWS, HEADS * HEAD), BF),
            jax.ShapeDtypeStruct((ROWS, HEAD), BF),
            jax.ShapeDtypeStruct((ROWS, HEAD), BF),
        ),
        in_specs=[hbm] * 5,
        out_specs=(anywhere,) * 4,
        scratch_shapes=[
            pltpu.VMEM((ROWS, HEADS * HEAD), BF),
            pltpu.VMEM((ROWS, HEAD), BF),
            pltpu.VMEM((ROWS, HEAD), BF),
            pltpu.VMEM((ROWS, HEADS * HEAD), BF),
            pltpu.VMEM((ROWS,), jnp.int32),
            pltpu.VMEM((STACKED, 2 * HEAD), BF),
            pltpu.VMEM((HEAD, ROWS), BF),
            pltpu.VMEM((HEAD, ROWS), BF),
            pltpu.VMEM((GROUPS, STACKED, WIDTH * TILE), BF),
            pltpu.VMEM((ROWS, HEADS * HEAD), BF),
            pltpu.VMEM((ROWS, HEADS * HEAD), BF),
            pltpu.VMEM((ROWS, HEAD), F32),
            pltpu.VMEM((ROWS, HEAD), F32),
            pltpu.VMEM((ROWS, HEAD), BF),
            pltpu.VMEM((ROWS, HEAD), BF),
            dma((BLOCKS,)),
            dma((BLOCKS,)),
            dma((3,)),
            dma((3,)),
            dma((3,)),
            dma,
            dma((BLOCKS,)),
            dma((2,)),
        ],
        compiler_params=pltpu.CompilerParams(
            collective_id=0, has_side_effects=True, vmem_limit_bytes=48 * 2**20
        ),
    )(queries, keys, values, output_gradient, doc_start)
    return pl.pallas_call(
        deliver,
        out_shape=tuple(jax.ShapeDtypeStruct(x.shape, x.dtype) for x in results),
        in_specs=[anywhere] * 4,
        out_specs=(hbm,) * 4,
        scratch_shapes=[dma((4, PIECES))],
        compiler_params=pltpu.CompilerParams(vmem_limit_bytes=VM2),
    )(*results)


def solution(mesh):
    return jax.shard_map(
        on_device,
        mesh=mesh,
        in_specs=(P("ctx", "tp"), P("ctx", "tp"), P("ctx", "tp"), P("ctx", "tp"), P("ctx")),
        out_specs=(P(("ctx", "tp"), None), P("ctx", "tp"), P("ctx", "tp"), P("ctx", "tp")),
        check_vma=False,
    )
```

time: 254 us -> 22.1 us (0.09)
  the two profiles are of different devices: /device:TPU:32 before, /device:TPU:1 now
where the time goes in v1:
time: 22.1 us; the launch traced here: 21.9 us
  Pallas kernels  21.3 us (96%)
  between operations  0.64 us (3%)
    pallas_call x1, Pallas kernels, on_device(): pl.pallas_call(kernel, out_shape=(jax.ShapeDtypeStruct((TILE, BLOCKS * HE...  19.9 us
    pallas_call x1, Pallas kernels, on_device(): pl.pallas_call(deliver, out_shape=tuple((jax.ShapeDtypeStruct(x.shape, x....  1.43 us

profile of v1, /device:TPU:1, one launch (start us, length us, event | category | flops | bytes accessed | tf_op | source)
XLA Modules:
  0.0 21.9 jit_solution(11712469103660829135)
XLA Ops:
  0.6 19.9 %shard_map.84 = (bf16[128,4096]{1,0:T(8,128)(2,1)S(1)}, bf16[512,1024]{1,0:T(8,128)(2,1)S(1)}, bf16[512,128]{1,0:T(8,128)(2,1)S(1)}, bf16[512,128]{1,0:T(8,128)(2,1)S(1)}) custom-call(bf16[512,1024]{1,0:T(8,128)(2,1)} %q_in.1, bf16[512,128]{1,0:T(8,128)(2,1)} %k_in.1, bf16[512,128]{1,0:T(8,128)(2,1)} %v_in.1, bf16[512,1024]{1,0:T(8,128)(2,1)} %g_in.1, ...), custom_call_target="tpu_custom_call" | custom-call | tf_op jit(solution)/shard_map/pallas_call | solution.py:214
  20.5 1.4 %shard_map.85 = (bf16[128,4096]{1,0:T(8,128)(2,1)}, bf16[512,1024]{1,0:T(8,128)(2,1)}, bf16[512,128]{1,0:T(8,128)(2,1)}, bf16[512,128]{1,0:T(8,128)(2,1)}) custom-call(bf16[128,4096]{1,0:T(8,128)(2,1)S(1)} %get-tuple-element.8.refs_0_, bf16[512,1024]{1,0:T(8,128)(2,1)S(1)} %get-tuple-element.9.refs_1_, bf16[512,128]{1,0:T(8,128)(2,1)S(1)} %get-tuple-element.10.refs_2_, ...), custom_call_target="tpu_custom_call" | custom-call | tf_op jit(solution)/shard_map/pallas_call | solution.py:253

commit v2 on v1

v2 whole, which is shorter than its diff:
```python
import functools
import math

import jax
import jax.numpy as jnp
from jax import lax
from jax.experimental import pallas as pl
from jax.experimental.pallas import tpu as pltpu
from jax.sharding import PartitionSpec as P

MESH = pl.DeviceIdType.MESH
BF, F32 = jnp.bfloat16, jnp.float32
NT = (((1,), (1,)), ((), ()))
NN = (((1,), (0,)), ((), ()))
HEAD = 128
TILE = 128
HEADS = 8
ROWS = 512
BLOCKS = 4
SCALE = 1.0 / math.sqrt(HEAD)
SCALE2 = math.log2(math.e) / math.sqrt(HEAD)
FIRST = (0, 128, 384, 768)
STACKED = 1280
ORDER = (2, 1, 3, 0)
PART = 4
PARTS = HEADS // PART


def head_cols(first, count=1):
    return pl.ds(pl.multiple_of(first * HEAD, HEAD), count * HEAD)


def stacked(ref, t, first, count):
    rows = slice(TILE * t, TILE * (t + 1))
    return [ref[rows, head_cols(first + x)] for x in range(count)]


def prepare(t, base, start, k, kaug):
    n, o = TILE * (t + 1), FIRST[t]
    kaug[o : o + n, 0:HEAD] = k[0:n, :]
    first = (start[pl.ds(TILE * t, TILE)] - base)[None, :]
    j = lax.broadcasted_iota(jnp.int32, (n, TILE), 0)
    i = lax.broadcasted_iota(jnp.int32, (n, TILE), 1) + TILE * t
    kaug[o : o + n, HEAD : 2 * HEAD] = jnp.where((j >= first) & (j <= i), 0.0, -1e30).astype(BF)


def forward(t, first, count, q, kaug, vt, prob, out):
    n, o = TILE * (t + 1), FIRST[t]
    eye = lax.broadcasted_iota(jnp.int32, (TILE, TILE), 0) == lax.broadcasted_iota(
        jnp.int32, (TILE, TILE), 1
    )
    eye = eye.astype(F32).astype(BF)
    queries = [jnp.concatenate([x, eye], 1) for x in stacked(q, t, first, count)]
    queries = jnp.concatenate(queries, 0)
    score = lax.dot_general(kaug[o : o + n, :], queries, NT, preferred_element_type=F32)
    top = jnp.max(score, axis=0, keepdims=True)
    expo = jnp.exp2((score - top) * SCALE2)
    prob_b = (expo * (1.0 / jnp.sum(expo, axis=0, keepdims=True))).astype(BF)
    prob[o : o + n, head_cols(first, count)] = prob_b
    out_t = lax.dot_general(vt[:, 0:n], prob_b, NN, preferred_element_type=F32)
    for x in range(count):
        out[TILE * t : TILE * (t + 1), head_cols(first + x)] = out_t[
            :, HEAD * x : HEAD * (x + 1)
        ].T.astype(BF)


def backward(t, q, g, v, kt, prob, dq, dk, dv):
    n, o = TILE * (t + 1), FIRST[t]
    queries = jnp.concatenate(stacked(q, t, 0, HEADS), 0)
    grads = jnp.concatenate(stacked(g, t, 0, HEADS), 0)
    prob_b = prob[o : o + n, :]
    dprob = lax.dot_general(v[0:n, :], grads, NT, preferred_element_type=F32)
    prob_f = prob_b.astype(F32)
    delta = jnp.sum(prob_f * dprob, axis=0, keepdims=True)
    dscore = (prob_f * (dprob - delta)).astype(BF)
    dq_t = lax.dot_general(kt[:, 0:n], dscore, NN, preferred_element_type=F32) * SCALE
    for x in range(HEADS):
        dq[TILE * t : TILE * (t + 1), head_cols(x)] = dq_t[:, HEAD * x : HEAD * (x + 1)].T.astype(
            BF
        )
    dk[0:n, :] += lax.dot_general(dscore, queries, NN, preferred_element_type=F32)
    dv[0:n, :] += lax.dot_general(prob_b, grads, NN, preferred_element_type=F32)


def kernel(
    q_in, k_in, v_in, g_in, start_in,
    att_out, dq_out, dk_out, dv_out,
    q, k, v, g, start, kaug, kt, vt, prob, out, dq, dk, dv, dk_b, dv_b,
    q_sem, g_sem, kv_sem, send_sem, recv_sem, own_sem, dq_sem, kv_out_sem,
):
    me = lax.axis_index("tp")
    base = lax.axis_index("ctx") * ROWS
    peers = [lax.rem(me + off, BLOCKS) for off in ORDER]

    def block(ref, t):
        return ref.at[pl.ds(pl.multiple_of(t * TILE, TILE), TILE)]

    def load(src, dst, sem):
        copy = pltpu.make_async_copy(src, dst, sem)
        copy.start()
        return copy

    k_load = load(k_in, k, kv_sem.at[0])
    q_loads = [load(block(q_in, peers[0]), block(q, peers[0]), q_sem.at[0])]
    start_load = load(start_in, start, kv_sem.at[1])
    v_load = load(v_in, v, kv_sem.at[2])
    barrier = pltpu.get_barrier_semaphore()
    for peer in peers[:3]:
        pl.semaphore_signal(barrier, inc=1, device_id={"tp": peer}, device_id_type=MESH)
    for i in range(1, BLOCKS):
        q_loads.append(load(block(q_in, peers[i]), block(q, peers[i]), q_sem.at[i]))
    mine = me * HEADS

    def send(i, first, count, slot):
        copy = pltpu.make_async_remote_copy(
            src_ref=block(out, peers[i]).at[:, head_cols(first, count)],
            dst_ref=att_out.at[:, head_cols(mine + first, count)],
            send_sem=send_sem.at[slot],
            recv_sem=recv_sem.at[slot],
            device_id={"tp": peers[i]},
            device_id_type=MESH,
        )
        copy.start()
        return copy

    def branch(i, body):
        lax.switch(peers[i], [functools.partial(body, t) for t in range(BLOCKS)])

    start_load.wait()
    k_load.wait()
    q_loads[0].wait()
    branch(0, lambda t: prepare(t, base, start, k, kaug))
    v_load.wait()
    vt[...] = v[...].T
    sends = []
    for part in range(PARTS):
        branch(0, lambda t: forward(t, part * PART, PART, q, kaug, vt, prob, out))
        if part == 0:
            pl.semaphore_wait(barrier, 3)
        sends.append(send(0, part * PART, PART, part))
    g_loads = [load(block(g_in, t), block(g, t), g_sem.at[t]) for t in range(BLOCKS)]

    def whole(t):
        prepare(t, base, start, k, kaug)
        forward(t, 0, HEADS, q, kaug, vt, prob, out)

    for i in range(1, BLOCKS):
        q_loads[i].wait()
        branch(i, whole)
        if i < 3:
            sends.append(send(i, 0, HEADS, PARTS + i - 1))
    own = pltpu.make_async_copy(block(out, me), att_out.at[:, head_cols(mine, HEADS)], own_sem)
    own.start()

    kt[...] = k[...].T
    dk[...] = jnp.zeros_like(dk)
    dv[...] = jnp.zeros_like(dv)
    for copy in g_loads:
        copy.wait()
    stores = []
    for t in range(BLOCKS):
        backward(t, q, g, v, kt, prob, dq, dk, dv)
        stores.append(
            pltpu.make_async_copy(
                dq.at[pl.ds(TILE * t, TILE)], dq_out.at[pl.ds(TILE * t, TILE)], dq_sem.at[t]
            )
        )
        stores[-1].start()
    dk_b[...] = (dk[...] * SCALE).astype(BF)
    dv_b[...] = dv[...].astype(BF)
    for i, (src, dst) in enumerate(((dk_b, dk_out), (dv_b, dv_out))):
        stores.append(pltpu.make_async_copy(src, dst, kv_out_sem.at[i]))
        stores[-1].start()
    for copy in stores:
        copy.wait()
    own.wait()
    for copy in sends:
        copy.wait()


def deliver(*refs):
    sems = refs[8]
    copies = [pltpu.make_async_copy(refs[i], refs[4 + i], sems.at[i]) for i in range(4)]
    for copy in copies:
        copy.start()
    for copy in copies:
        copy.wait()


def on_device(queries, keys, values, output_gradient, doc_start):
    anywhere = pl.BlockSpec(memory_space=pl.ANY)
    hbm = pl.BlockSpec(memory_space=pltpu.HBM)
    dma = pltpu.SemaphoreType.DMA
    queries, keys, values, output_gradient, doc_start = (
        pltpu.with_memory_space_constraint(x, pltpu.HBM)
        for x in (queries, keys, values, output_gradient, doc_start)
    )
    results = pl.pallas_call(
        kernel,
        out_shape=(
            jax.ShapeDtypeStruct((TILE, BLOCKS * HEADS * HEAD), BF),
            jax.ShapeDtypeStruct((ROWS, HEADS * HEAD), BF),
            jax.ShapeDtypeStruct((ROWS, HEAD), BF),
            jax.ShapeDtypeStruct((ROWS, HEAD), BF),
        ),
        in_specs=[hbm] * 5,
        out_specs=(anywhere,) * 4,
        scratch_shapes=[
            pltpu.VMEM((ROWS, HEADS * HEAD), BF),
            pltpu.VMEM((ROWS, HEAD), BF),
            pltpu.VMEM((ROWS, HEAD), BF),
            pltpu.VMEM((ROWS, HEADS * HEAD), BF),
            pltpu.VMEM((ROWS,), jnp.int32),
            pltpu.VMEM((STACKED, 2 * HEAD), BF),
            pltpu.VMEM((HEAD, ROWS), BF),
            pltpu.VMEM((HEAD, ROWS), BF),
            pltpu.VMEM((STACKED, HEADS * TILE), BF),
            pltpu.VMEM((ROWS, HEADS * HEAD), BF),
            pltpu.VMEM((ROWS, HEADS * HEAD), BF),
            pltpu.VMEM((ROWS, HEAD), F32),
            pltpu.VMEM((ROWS, HEAD), F32),
            pltpu.VMEM((ROWS, HEAD), BF),
            pltpu.VMEM((ROWS, HEAD), BF),
            dma((BLOCKS,)),
            dma((BLOCKS,)),
            dma((3,)),
            dma((PARTS + 2,)),
            dma((PARTS + 2,)),
            dma,
            dma((BLOCKS,)),
            dma((2,)),
        ],
        compiler_params=pltpu.CompilerParams(
            collective_id=0, has_side_effects=True, vmem_limit_bytes=48 * 2**20
        ),
    )(queries, keys, values, output_gradient, doc_start)
    return pl.pallas_call(
        deliver,
        out_shape=tuple(jax.ShapeDtypeStruct(x.shape, x.dtype) for x in results),
        in_specs=[anywhere] * 4,
        out_specs=(hbm,) * 4,
        scratch_shapes=[dma((4,))],
        compiler_params=pltpu.CompilerParams(vmem_limit_bytes=2**20),
    )(*results)


def solution(mesh):
    return jax.shard_map(
        on_device,
        mesh=mesh,
        in_specs=(P("ctx", "tp"), P("ctx", "tp"), P("ctx", "tp"), P("ctx", "tp"), P("ctx")),
        out_specs=(P(("ctx", "tp"), None), P("ctx", "tp"), P("ctx", "tp"), P("ctx", "tp")),
        check_vma=False,
    )
```

time: 22.1 us -> 20.2 us (0.914)
  the two profiles are of different devices: /device:TPU:1 before, /device:TPU:497 now
where the time goes in v2:
time: 20.2 us; the launch traced here: 20.1 us
  Pallas kernels  19.3 us (96%)
  between operations  0.8 us (4%)
    pallas_call x1, Pallas kernels, on_device(): pl.pallas_call(kernel, out_shape=(jax.ShapeDtypeStruct((TILE, BLOCKS * HE...  17.8 us
    pallas_call x1, Pallas kernels, on_device(): pl.pallas_call(deliver, out_shape=tuple((jax.ShapeDtypeStruct(x.shape, x....  1.43 us

profile of v2, /device:TPU:497, one launch (start us, length us, event | category | flops | bytes accessed | tf_op | source)
XLA Modules:
  0.0 20.1 jit_solution(17845531461634265503)
XLA Ops:
  0.6 17.8 %shard_map.84 = (bf16[128,4096]{1,0:T(8,128)(2,1)S(1)}, bf16[512,1024]{1,0:T(8,128)(2,1)S(1)}, bf16[512,128]{1,0:T(8,128)(2,1)S(1)}, bf16[512,128]{1,0:T(8,128)(2,1)S(1)}) custom-call(bf16[512,1024]{1,0:T(8,128)(2,1)} %q_in.1, bf16[512,128]{1,0:T(8,128)(2,1)} %k_in.1, bf16[512,128]{1,0:T(8,128)(2,1)} %v_in.1, bf16[512,1024]{1,0:T(8,128)(2,1)} %g_in.1, ...), custom_call_target="tpu_custom_call" | custom-call | tf_op jit(solution)/shard_map/pallas_call | solution.py:198
  18.5 1.4 %shard_map.85 = (bf16[128,4096]{1,0:T(8,128)(2,1)}, bf16[512,1024]{1,0:T(8,128)(2,1)}, bf16[512,128]{1,0:T(8,128)(2,1)}, bf16[512,128]{1,0:T(8,128)(2,1)}) custom-call(bf16[128,4096]{1,0:T(8,128)(2,1)S(1)} %get-tuple-element.8.refs_0_, bf16[512,1024]{1,0:T(8,128)(2,1)S(1)} %get-tuple-element.9.refs_1_, bf16[512,128]{1,0:T(8,128)(2,1)S(1)} %get-tuple-element.10.refs_2_, ...), custom_call_target="tpu_custom_call" | custom-call | tf_op jit(solution)/shard_map/pallas_call | solution.py:237

commit v3 on v2

--- a/solution.py
+++ b/solution.py
@@ -35,24 +35,20 @@
     return [ref[rows, head_cols(first + x)] for x in range(count)]
 
 
-def prepare(t, base, start, k, kaug):
+def make_masks(base, start, masks):
+    for t in range(BLOCKS):
+        n, o = TILE * (t + 1), FIRST[t]
+        first = (start[pl.ds(TILE * t, TILE)] - base)[None, :]
+        j = lax.broadcasted_iota(jnp.int32, (n, TILE), 0)
+        i = lax.broadcasted_iota(jnp.int32, (n, TILE), 1) + TILE * t
+        masks[o : o + n, :] = jnp.where((j >= first) & (j <= i), 0.0, -1e30)
+
+
+def forward(t, first, count, q, k, masks, vt, prob, out):
     n, o = TILE * (t + 1), FIRST[t]
-    kaug[o : o + n, 0:HEAD] = k[0:n, :]
-    first = (start[pl.ds(TILE * t, TILE)] - base)[None, :]
-    j = lax.broadcasted_iota(jnp.int32, (n, TILE), 0)
-    i = lax.broadcasted_iota(jnp.int32, (n, TILE), 1) + TILE * t
-    kaug[o : o + n, HEAD : 2 * HEAD] = jnp.where((j >= first) & (j <= i), 0.0, -1e30).astype(BF)
-
-
-def forward(t, first, count, q, kaug, vt, prob, out):
-    n, o = TILE * (t + 1), FIRST[t]
-    eye = lax.broadcasted_iota(jnp.int32, (TILE, TILE), 0) == lax.broadcasted_iota(
-        jnp.int32, (TILE, TILE), 1
-    )
-    eye = eye.astype(F32).astype(BF)
-    queries = [jnp.concatenate([x, eye], 1) for x in stacked(q, t, first, count)]
-    queries = jnp.concatenate(queries, 0)
-    score = lax.dot_general(kaug[o : o + n, :], queries, NT, preferred_element_type=F32)
+    queries = jnp.concatenate(stacked(q, t, first, count), 0)
+    score = lax.dot_general(k[0:n, :], queries, NT, preferred_element_type=F32)
+    score += jnp.concatenate([masks[o : o + n, :]] * count, 1)
     top = jnp.max(score, axis=0, keepdims=True)
     expo = jnp.exp2((score - top) * SCALE2)
     prob_b = (expo * (1.0 / jnp.sum(expo, axis=0, keepdims=True))).astype(BF)
@@ -85,8 +81,8 @@
 def kernel(
     q_in, k_in, v_in, g_in, start_in,
     att_out, dq_out, dk_out, dv_out,
-    q, k, v, g, start, kaug, kt, vt, prob, out, dq, dk, dv, dk_b, dv_b,
-    q_sem, g_sem, kv_sem, send_sem, recv_sem, own_sem, dq_sem, kv_out_sem,
+    q, k, v, g, start, masks, kt, vt, prob, out, dq, dk, dv, dk_b, dv_b,
+    sems, send_sem, recv_sem,
 ):
     me = lax.axis_index("tp")
     base = lax.axis_index("ctx") * ROWS
@@ -95,87 +91,85 @@
     def block(ref, t):
         return ref.at[pl.ds(pl.multiple_of(t * TILE, TILE), TILE)]
 
-    def load(src, dst, sem):
+    def move(src, dst, sem):
         copy = pltpu.make_async_copy(src, dst, sem)
         copy.start()
         return copy
 
-    k_load = load(k_in, k, kv_sem.at[0])
-    q_loads = [load(block(q_in, peers[0]), block(q, peers[0]), q_sem.at[0])]
-    start_load = load(start_in, start, kv_sem.at[1])
-    v_load = load(v_in, v, kv_sem.at[2])
+    k_load = move(k_in, k, sems.at[0])
+    q_load = move(block(q_in, peers[0]), block(q, peers[0]), sems.at[1])
+    start_load = move(start_in, start, sems.at[2])
+    v_load = move(v_in, v, sems.at[3])
     barrier = pltpu.get_barrier_semaphore()
     for peer in peers[:3]:
         pl.semaphore_signal(barrier, inc=1, device_id={"tp": peer}, device_id_type=MESH)
     for i in range(1, BLOCKS):
-        q_loads.append(load(block(q_in, peers[i]), block(q, peers[i]), q_sem.at[i]))
+        move(block(q_in, peers[i]), block(q, peers[i]), sems.at[4])
     mine = me * HEADS
 
-    def send(i, first, count, slot):
-        copy = pltpu.make_async_remote_copy(
+    def send(i, first, count):
+        pltpu.make_async_remote_copy(
             src_ref=block(out, peers[i]).at[:, head_cols(first, count)],
             dst_ref=att_out.at[:, head_cols(mine + first, count)],
-            send_sem=send_sem.at[slot],
-            recv_sem=recv_sem.at[slot],
+            send_sem=send_sem,
+            recv_sem=recv_sem,
             device_id={"tp": peers[i]},
             device_id_type=MESH,
-        )
-        copy.start()
-        return copy
+        ).start()
+
+    def arrived(ref, sem):
+        pltpu.make_async_copy(ref, ref, sem).wait()
 
     def branch(i, body):
         lax.switch(peers[i], [functools.partial(body, t) for t in range(BLOCKS)])
 
     start_load.wait()
+    make_masks(base, start, masks)
     k_load.wait()
-    q_loads[0].wait()
-    branch(0, lambda t: prepare(t, base, start, k, kaug))
+    q_load.wait()
     v_load.wait()
-    vt[...] = v[...].T
-    sends = []
+
+    def partial(part, t):
+        if part == 0:
+            vt[...] = v[...].T
+        forward(t, part * PART, PART, q, k, masks, vt, prob, out)
+
     for part in range(PARTS):
-        branch(0, lambda t: forward(t, part * PART, PART, q, kaug, vt, prob, out))
+        branch(0, functools.partial(partial, part))
         if part == 0:
             pl.semaphore_wait(barrier, 3)
-        sends.append(send(0, part * PART, PART, part))
-    g_loads = [load(block(g_in, t), block(g, t), g_sem.at[t]) for t in range(BLOCKS)]
+        send(0, part * PART, PART)
+    g_load = move(g_in, g, sems.at[5])
 
     def whole(t):
-        prepare(t, base, start, k, kaug)
-        forward(t, 0, HEADS, q, kaug, vt, prob, out)
-
+        forward(t, 0, HEADS, q, k, masks, vt, prob, out)
+
+    others = pl.ds(0, (BLOCKS - 1) * TILE)
+    arrived(q.at[others], sems.at[4])
     for i in range(1, BLOCKS):
-        q_loads[i].wait()
         branch(i, whole)
         if i < 3:
-            sends.append(send(i, 0, HEADS, PARTS + i - 1))
-    own = pltpu.make_async_copy(block(out, me), att_out.at[:, head_cols(mine, HEADS)], own_sem)
-    own.start()
+            send(i, 0, HEADS)
+    own = move(block(out, me), att_out.at[:, head_cols(mine, HEADS)], sems.at[1])
 
     kt[...] = k[...].T
     dk[...] = jnp.zeros_like(dk)
     dv[...] = jnp.zeros_like(dv)
-    for copy in g_loads:
-        copy.wait()
-    stores = []
+    g_load.wait()
     for t in range(BLOCKS):
         backward(t, q, g, v, kt, prob, dq, dk, dv)
-        stores.append(
-            pltpu.make_async_copy(
-                dq.at[pl.ds(TILE * t, TILE)], dq_out.at[pl.ds(TILE * t, TILE)], dq_sem.at[t]
-            )
-        )
-        stores[-1].start()
     dk_b[...] = (dk[...] * SCALE).astype(BF)
     dv_b[...] = dv[...].astype(BF)
-    for i, (src, dst) in enumerate(((dk_b, dk_out), (dv_b, dv_out))):
-        stores.append(pltpu.make_async_copy(src, dst, kv_out_sem.at[i]))
-        stores[-1].start()
+    stores = [
+        move(dq, dq_out, sems.at[0]),
+        move(dk_b, dk_out, sems.at[2]),
+        move(dv_b, dv_out, sems.at[3]),
+        own,
+    ]
     for copy in stores:
         copy.wait()
-    own.wait()
-    for copy in sends:
-        copy.wait()
+    arrived(out.at[others], send_sem)
+    arrived(att_out.at[:, head_cols(0, (BLOCKS - 1) * HEADS)], recv_sem)
 
 
 def deliver(*refs):
@@ -211,7 +205,7 @@
             pltpu.VMEM((ROWS, HEAD), BF),
             pltpu.VMEM((ROWS, HEADS * HEAD), BF),
             pltpu.VMEM((ROWS,), jnp.int32),
-            pltpu.VMEM((STACKED, 2 * HEAD), BF),
+            pltpu.VMEM((STACKED, TILE), F32),
             pltpu.VMEM((HEAD, ROWS), BF),
             pltpu.VMEM((HEAD, ROWS), BF),
             pltpu.VMEM((STACKED, HEADS * TILE), BF),
@@ -221,14 +215,9 @@
             pltpu.VMEM((ROWS, HEAD), F32),
             pltpu.VMEM((ROWS, HEAD), BF),
             pltpu.VMEM((ROWS, HEAD), BF),
-            dma((BLOCKS,)),
-            dma((BLOCKS,)),
-            dma((3,)),
-            dma((PARTS + 2,)),
-            dma((PARTS + 2,)),
+            dma((6,)),
             dma,
-            dma((BLOCKS,)),
-            dma((2,)),
+            dma,
         ],
         compiler_params=pltpu.CompilerParams(
             collective_id=0, has_side_effects=True, vmem_limit_bytes=48 * 2**20

time: 20.2 us -> 19.9 us (0.985)
  the two profiles are of different devices: /device:TPU:497 before, /device:TPU:481 now
where the time goes in v3:
time: 19.9 us; the launch traced here: 19.7 us
  Pallas kernels  18.9 us (95%)
  between operations  0.8 us (4%)
    pallas_call x1, Pallas kernels, on_device(): pl.pallas_call(kernel, out_shape=(jax.ShapeDtypeStruct((TILE, BLOCKS * HE...  17.5 us
    pallas_call x1, Pallas kernels, on_device(): pl.pallas_call(deliver, out_shape=tuple((jax.ShapeDtypeStruct(x.shape, x....  1.43 us

profile of v3, /device:TPU:481, one launch (start us, length us, event | category | flops | bytes accessed | tf_op | source)
XLA Modules:
  0.0 19.7 jit_solution(6407995717890890879)
XLA Ops:
  0.6 17.5 %shard_map.84 = (bf16[128,4096]{1,0:T(8,128)(2,1)S(1)}, bf16[512,1024]{1,0:T(8,128)(2,1)S(1)}, bf16[512,128]{1,0:T(8,128)(2,1)S(1)}, bf16[512,128]{1,0:T(8,128)(2,1)S(1)}) custom-call(bf16[512,1024]{1,0:T(8,128)(2,1)} %q_in.1, bf16[512,128]{1,0:T(8,128)(2,1)} %k_in.1, bf16[512,128]{1,0:T(8,128)(2,1)} %v_in.1, bf16[512,1024]{1,0:T(8,128)(2,1)} %g_in.1, ...), custom_call_target="tpu_custom_call" | custom-call | tf_op jit(solution)/shard_map/pallas_call | solution.py:192
  18.1 1.4 %shard_map.85 = (bf16[128,4096]{1,0:T(8,128)(2,1)}, bf16[512,1024]{1,0:T(8,128)(2,1)}, bf16[512,128]{1,0:T(8,128)(2,1)}, bf16[512,128]{1,0:T(8,128)(2,1)}) custom-call(bf16[128,4096]{1,0:T(8,128)(2,1)S(1)} %get-tuple-element.8.refs_0_, bf16[512,1024]{1,0:T(8,128)(2,1)S(1)} %get-tuple-element.9.refs_1_, bf16[512,128]{1,0:T(8,128)(2,1)S(1)} %get-tuple-element.10.refs_2_, ...), custom_call_target="tpu_custom_call" | custom-call | tf_op jit(solution)/shard_map/pallas_call | solution.py:226

commit v4 on v3

--- a/solution.py
+++ b/solution.py
@@ -51,9 +51,10 @@
     score += jnp.concatenate([masks[o : o + n, :]] * count, 1)
     top = jnp.max(score, axis=0, keepdims=True)
     expo = jnp.exp2((score - top) * SCALE2)
-    prob_b = (expo * (1.0 / jnp.sum(expo, axis=0, keepdims=True))).astype(BF)
-    prob[o : o + n, head_cols(first, count)] = prob_b
-    out_t = lax.dot_general(vt[:, 0:n], prob_b, NN, preferred_element_type=F32)
+    out_t = lax.dot_general(vt[:, 0:n], expo.astype(BF), NN, preferred_element_type=F32)
+    share = 1.0 / jnp.sum(expo, axis=0, keepdims=True)
+    out_t = out_t * share
+    prob[o : o + n, head_cols(first, count)] = (expo * share).astype(BF)
     for x in range(count):
         out[TILE * t : TILE * (t + 1), head_cols(first + x)] = out_t[
             :, HEAD * x : HEAD * (x + 1)
@@ -96,15 +97,22 @@
         copy.start()
         return copy
 
-    k_load = move(k_in, k, sems.at[0])
-    q_load = move(block(q_in, peers[0]), block(q, peers[0]), sems.at[1])
-    start_load = move(start_in, start, sems.at[2])
-    v_load = move(v_in, v, sems.at[3])
+    for t in range(BLOCKS):
+        move(block(k_in, t), block(k, t), sems.at[0])
+    for x in range(HEADS):
+        move(
+            block(q_in, peers[0]).at[:, head_cols(x)],
+            block(q, peers[0]).at[:, head_cols(x)],
+            sems.at[0],
+        )
+    start_load = move(start_in, start, sems.at[1])
+    for t in range(BLOCKS):
+        move(block(v_in, t), block(v, t), sems.at[0])
     barrier = pltpu.get_barrier_semaphore()
     for peer in peers[:3]:
         pl.semaphore_signal(barrier, inc=1, device_id={"tp": peer}, device_id_type=MESH)
     for i in range(1, BLOCKS):
-        move(block(q_in, peers[i]), block(q, peers[i]), sems.at[4])
+        move(block(q_in, peers[i]), block(q, peers[i]), sems.at[2])
     mine = me * HEADS
 
     def send(i, first, count):
@@ -125,9 +133,7 @@
 
     start_load.wait()
     make_masks(base, start, masks)
-    k_load.wait()
-    q_load.wait()
-    v_load.wait()
+    arrived(q.at[pl.ds(0, 2 * TILE)], sems.at[0])
 
     def partial(part, t):
         if part == 0:
@@ -139,18 +145,18 @@
         if part == 0:
             pl.semaphore_wait(barrier, 3)
         send(0, part * PART, PART)
-    g_load = move(g_in, g, sems.at[5])
+    g_load = move(g_in, g, sems.at[3])
 
     def whole(t):
         forward(t, 0, HEADS, q, k, masks, vt, prob, out)
 
     others = pl.ds(0, (BLOCKS - 1) * TILE)
-    arrived(q.at[others], sems.at[4])
+    arrived(q.at[others], sems.at[2])
     for i in range(1, BLOCKS):
         branch(i, whole)
         if i < 3:
             send(i, 0, HEADS)
-    own = move(block(out, me), att_out.at[:, head_cols(mine, HEADS)], sems.at[1])
+    move(block(out, me), att_out.at[:, head_cols(mine, HEADS)], sems.at[0])
 
     kt[...] = k[...].T
     dk[...] = jnp.zeros_like(dk)
@@ -160,14 +166,10 @@
         backward(t, q, g, v, kt, prob, dq, dk, dv)
     dk_b[...] = (dk[...] * SCALE).astype(BF)
     dv_b[...] = dv[...].astype(BF)
-    stores = [
-        move(dq, dq_out, sems.at[0]),
-        move(dk_b, dk_out, sems.at[2]),
-        move(dv_b, dv_out, sems.at[3]),
-        own,
-    ]
-    for copy in stores:
-        copy.wait()
+    move(dq, dq_out, sems.at[0])
+    move(dk_b, dk_out, sems.at[0])
+    move(dv_b, dv_out, sems.at[0])
+    arrived(prob.at[pl.ds(0, 6 * TILE)], sems.at[0])
     arrived(out.at[others], send_sem)
     arrived(att_out.at[:, head_cols(0, (BLOCKS - 1) * HEADS)], recv_sem)
 
@@ -215,7 +217,7 @@
             pltpu.VMEM((ROWS, HEAD), F32),
             pltpu.VMEM((ROWS, HEAD), BF),
             pltpu.VMEM((ROWS, HEAD), BF),
-            dma((6,)),
+            dma((4,)),
             dma,
             dma,
         ],

time: 19.9 us -> 19.8 us (level)
  the two profiles are of different devices: /device:TPU:481 before, /device:TPU:385 now
where the time goes in v4:
time: 19.8 us; the launch traced here: 19.6 us
  Pallas kernels  18.8 us (95%)
  between operations  0.8 us (4%)
    pallas_call x1, Pallas kernels, on_device(): pl.pallas_call(kernel, out_shape=(jax.ShapeDtypeStruct((TILE, BLOCKS * HE...  17.4 us
    pallas_call x1, Pallas kernels, on_device(): pl.pallas_call(deliver, out_shape=tuple((jax.ShapeDtypeStruct(x.shape, x....  1.43 us

profile of v4, /device:TPU:385, one launch (start us, length us, event | category | flops | bytes accessed | tf_op | source)
XLA Modules:
  0.0 19.6 jit_solution(11724433327388037418)
XLA Ops:
  0.6 17.4 %shard_map.84 = (bf16[128,4096]{1,0:T(8,128)(2,1)S(1)}, bf16[512,1024]{1,0:T(8,128)(2,1)S(1)}, bf16[512,128]{1,0:T(8,128)(2,1)S(1)}, bf16[512,128]{1,0:T(8,128)(2,1)S(1)}) custom-call(bf16[512,1024]{1,0:T(8,128)(2,1)} %q_in.1, bf16[512,128]{1,0:T(8,128)(2,1)} %k_in.1, bf16[512,128]{1,0:T(8,128)(2,1)} %v_in.1, bf16[512,1024]{1,0:T(8,128)(2,1)} %g_in.1, ...), custom_call_target="tpu_custom_call" | custom-call | tf_op jit(solution)/shard_map/pallas_call | solution.py:194
  18.0 1.4 %shard_map.85 = (bf16[128,4096]{1,0:T(8,128)(2,1)}, bf16[512,1024]{1,0:T(8,128)(2,1)}, bf16[512,128]{1,0:T(8,128)(2,1)}, bf16[512,128]{1,0:T(8,128)(2,1)}) custom-call(bf16[128,4096]{1,0:T(8,128)(2,1)S(1)} %get-tuple-element.8.refs_0_, bf16[512,1024]{1,0:T(8,128)(2,1)S(1)} %get-tuple-element.9.refs_1_, bf16[512,128]{1,0:T(8,128)(2,1)S(1)} %get-tuple-element.10.refs_2_, ...), custom_call_target="tpu_custom_call" | custom-call | tf_op jit(solution)/shard_map/pallas_call | solution.py:228
